TPU v7x, 512 devices: a whole 4x8x8 slice. The times are simulated.
512 devices in a mesh: rows: 32 (over x, y), depth: 16 (over z, core).
Axes of the slice: x: 4, y: 8, z: 8, core: 2. Of those that a mesh axis runs over, the one named last changes fastest.
Arguments:
- left_factors: bfloat16 [32, 32, 2048, 128], P('rows', 'depth'), may hold values from -0.125 to 0.125
- right_factors: bfloat16 [32, 32, 2048, 128], P('rows', 'depth'), may hold values from -0.125 to 0.125
- probe_matrix: bfloat16 [2048, 128], replicated, may hold values from -6 to 6
- tile_list: int32 [32, 4], replicated, may hold values from 0 to 31, all different within a row
Outputs:
- basis: float32 [32, 4, 2048, 128], P('rows', None, 'depth')
- chol_factor: float32 [32, 4, 128, 128], P('rows')
Inputs may be any that keep to these rules, and one draw needn't show every extreme that they name: `tile_list`: each row holds 4 different tile rows, and every tile row is named by some row.
All inputs are finite; a program needn't handle non-finite values.
Results may differ from a plain program's by a relative error of at most 0.0058.
Values may be sent and summed in bfloat16 or wider, within the bound.
A program may use at most 64 MiB of HBM per device.

v0:
```python
import math

import jax
import jax.numpy as jnp
from jax import lax
from jax.sharding import PartitionSpec as P


def on_device(left_factors, right_factors, probe_matrix, tile_list):
    left_own = left_factors[0]
    right_own = right_factors[0]
    panels, tile_size, rank_size = left_own.shape
    scale = math.sqrt(float(tile_size))
    image = jnp.einsum(
        "pbk,bl->pkl", left_own, probe_matrix, preferred_element_type=jnp.float32
    ).astype(jnp.bfloat16)
    sketch_rows = jnp.einsum(
        "pbk,pkl->pbl", right_own, image, preferred_element_type=jnp.float32
    ).astype(jnp.bfloat16)
    sliced = lax.all_to_all(sketch_rows[:, None], "rows", split_axis=2, concat_axis=1, tiled=True)
    readers_order = jnp.transpose(tile_list)
    outgoing = jnp.take(sliced, readers_order, axis=1)
    arrived = lax.all_to_all(outgoing, "rows", split_axis=2, concat_axis=2, tiled=True)
    listed = arrived.shape[1]
    arrived = arrived.reshape(panels, listed, tile_size, rank_size)
    coupling = jnp.einsum(
        "pbk,ptbl->tpkl", right_own, arrived, preferred_element_type=jnp.float32
    ).astype(jnp.bfloat16)
    partial_sketch = jnp.einsum(
        "pbk,tpkl->tbl", left_own, coupling, preferred_element_type=jnp.float32
    )
    block_rows = tile_size // lax.axis_size("depth")
    total = lax.psum(partial_sketch, "depth")
    gram = jnp.einsum("tbk,tbl->tkl", total, total, precision=lax.Precision.HIGHEST)
    start = lax.axis_index("depth") * block_rows
    own_rows = lax.dynamic_slice_in_dim(total, start, block_rows, 1)
    lower = jnp.linalg.cholesky(gram)
    solved = jax.scipy.linalg.solve_triangular(
        lower, jnp.transpose(own_rows, (0, 2, 1)), lower=True
    )
    basis = jnp.transpose(solved, (0, 2, 1)) * scale
    return (basis[None], (lower / scale)[None])


def solution(mesh):
    in_specs = (P("rows", "depth", None, None), P("rows", "depth", None, None), P(), P())
    out_specs = (P("rows", None, "depth", None), P("rows", None, None, None))
    return jax.shard_map(
        on_device, mesh=mesh, in_specs=in_specs, out_specs=out_specs, check_vma=False
    )
```

profile of v0, /device:TPU:1, one launch (start us, length us, event | category | flops | bytes accessed | tf_op | source)
XLA Modules:
  0.0 398.3 jit_solution(8953928017421091047)
XLA Ops:
  7.2 0.0 copy-start
  7.2 1.2 copy-done
  8.4 2.3 fusion.3
  10.7 2.0 copy.31
  12.7 10.5 %all-to-all-start = ((bf16[2,1,2048,128]{3,0,1,2:T(2,128)(2,1)}), bf16[2,1,2048,128]{3,0,1,2:T(2,128)(2,1)S(1)}, u32[]{:S(2)}, u32[]{:S(2)}) async-start(bf16[2,1,2048,128]{3,0,1,2:T(2,128)(2,1)} %copy.31), calls=%async_computation | async-start | bytes 2097152 | tf_op jit(solution)/shard_map/all_to_all | solution.py:20
  23.2 0.0 all-reduce.2.cloned.1.call-start
  23.3 0.1 reshape.29
  23.4 0.1 copy.28
  23.5 24.3 %all-to-all-done = bf16[2,1,2048,128]{3,0,1,2:T(2,128)(2,1)S(1)} async-done(((bf16[2,1,2048,128]{3,0,1,2:T(2,128)(2,1)}), bf16[2,1,2048,128]{3,0,1,2:T(2,128)(2,1)S(1)}, u32[]{:S(2)}, u32[]{:S(2)}) %all-to-all-start) | async-done | bytes 1048608 | tf_op jit(solution)/shard_map/all_to_all | solution.py:20
  47.8 0.1 copy.32
  48.0 3.0 gather_fusion
  51.0 2.5 fusion.2
  53.5 100.6 %all_to_all.17 = bf16[2,4,32,64,128]{4,3,1,0,2:T(8,128)(2,1)S(1)} all-to-all(bf16[2,4,32,64,128]{4,3,1,0,2:T(8,128)(2,1)S(1)} %fusion.2), channel_id=1, replica_groups=mesh['rows'=32,'depth'=16] {'rows'}, dimensions={2} | all-to-all | bytes 8388608 | tf_op jit(solution)/shard_map/all_to_all | solution.py:23
  154.1 2.9 copy.34
  157.0 6.1 %convolution_bitcast_fusion = f32[4,2048,128]{1,2,0:T(8,128)} fusion(bf16[1,2,2048,128]{3,2,1,0:T(8,128)(2,1)S(1)} %copy-done, bf16[2,4,2048,128]{3,2,1,0:T(8,128)(2,1)} %bitcast.58, bf16[1,2,2048,128]{3,2,1,0:T(8,128)(2,1)S(1)} %copy-done.1), kind=kOutput, calls=%fused_computation.5 | convolution fusion | flops 1073872896 | bytes 10485760 | tf_op jit(solution)/shard_map/pbk,tpkl->tbl/dot_general | solution.py:29
  163.2 0.0 all-reduce.2.cloned.1.call-update
  163.2 131.2 %all-reduce.2.cloned.1.call-done = f32[4,2048,128]{1,2,0:T(8,128)} async-done(((f32[4,2048,128]{1,2,0:T(8,128)}), f32[4,2048,128]{1,2,0:T(8,128)}) %all-reduce.2.cloned.1.call-update) | async-done | bytes 4194320 | tf_op jit(solution)/shard_map/psum | solution.py:33
  294.5 7.4 %fusion.26 = f32[4,128,128]{2,1,0:T(8,128)S(1)} fusion(f32[4,2048,128]{1,2,0:T(8,128)} %all-reduce.2.cloned.1.call-done), kind=kOutput, calls=%fused_computation.33 | convolution fusion | flops 1610612736 | bytes 4456448 | tf_op jit(solution)/shard_map/tbk,tbl->tkl/dot_general | solution.py:34
  301.9 0.1 copy.37
  302.0 46.9 %custom-call.8 = f32[4,128,128]{2,1,0:T(8,128)S(1)} custom-call(f32[4,128,128]{2,1,0:T(8,128)S(1)} %fusion.23), custom_call_target="Cholesky" | custom-call | tf_op jit(solution)/shard_map/jit(cholesky)/cholesky | solution.py:37
  349.0 0.1 compare_reduce_fusion
  349.1 0.8 multiply_bitcast_fusion
  349.9 39.3 %custom-call.9 = f32[4,1,128,128]{2,3,1,0:T(8,128)S(1)} custom-call(f32[4,1,128,128]{3,2,1,0:T(8,128)S(1)} %get-tuple-element.3), custom_call_target="InvertDiagBlocksLowerTriangular" | custom-call | tf_op jit(solution)/shard_map/jit(_solve_triangular)/vmap()/triangular_solve | solution.py:38
  389.2 2.3 fusion.10
  (11 shorter events, 0.1 us)
Async XLA Ops:
  7.2 1.2 copy-start
  8.4 14.8 %copy-start.2 = (s32[32,4]{0,1:T(4,128)S(1)}, s32[32,4]{0,1:T(4,128)}, u32[]{:S(2)}) copy-start(s32[32,4]{0,1:T(4,128)} %param.7) | copy-start | bytes 1540
  12.7 35.1 %all-to-all-start = ((bf16[2,1,2048,128]{3,0,1,2:T(2,128)(2,1)}), bf16[2,1,2048,128]{3,0,1,2:T(2,128)(2,1)S(1)}, u32[]{:S(2)}, u32[]{:S(2)}) async-start(bf16[2,1,2048,128]{3,0,1,2:T(2,128)(2,1)} %copy.31), calls=%async_computation | async-start | bytes 2097152 | tf_op jit(solution)/shard_map/all_to_all | solution.py:20
  23.2 271.3 %all-reduce.2.cloned.1.call-start = ((), (), s32[]{:S(2)}) async-start(), calls=%async_computation.2 | async-start | bytes 8388608 | tf_op jit(solution)/shard_map/psum | solution.py:33
  154.1 3.0 copy-start.1
Sparse Core Ops, SparseCore 0:
  163.3 131.1 all-reduce.1
where the time goes:
time: 399 us; the launch traced here: 398 us
  waiting for transfers between devices  156 us (39%)
  blocking collectives  101 us (25%)
  other arithmetic  89.8 us (23%)
  matrix products  18.1 us (5%)
  between operations  14.1 us (4%)
  starting transfers between devices  10.5 us (3%)
  local copies, waits for them, and re-layouts  9.65 us (2%)
    psum x1, waiting for transfers between devices, on_device(): total = lax.psum(partial_sketch, 'depth')  131 us
    all_to_all x1, blocking collectives, on_device(): lax.all_to_all(outgoing, 'rows', split_axis=2, concat_axis=2, tiled=True)  101 us
    another operation x4, other arithmetic, on_device(): lower = jnp.linalg.cholesky(gram)  47.1 us
    another operation x2, other arithmetic, on_device(): jax.scipy.linalg.solve_triangular(lower, jnp.transpose(own_rows, (0, 2, 1...  39.3 us
    all_to_all x1, waiting for transfers between devices, on_device(): lax.all_to_all(sketch_rows[:, None], 'rows', split_axis=2, concat_axis=1,...  24.3 us
    all_to_all x1, starting transfers between devices, on_device(): lax.all_to_all(sketch_rows[:, None], 'rows', split_axis=2, concat_axis=1,...  10.5 us
  transfers between devices with their start and end apart: 2, of which 2 were waited for; matrix products, arithmetic and copies ran while one was open for 0% of the time, Pallas kernels for 0%

commit v1 on v0

v1 whole, which is shorter than its diff:
```python
import functools
import math

import jax
import jax.numpy as jnp
from jax import lax
from jax.experimental import pallas as pl
from jax.experimental.pallas import tpu as pltpu
from jax.sharding import PartitionSpec as P

MESH = pl.DeviceIdType.MESH
F32 = jnp.float32
BF16 = jnp.bfloat16
XS = 4
CORES = 2
HIGHEST = lax.Precision.HIGHEST


def spiral(count):
    order = [0]
    for step in range(1, count // 2 + 1):
        order.append(step)
        if count - step != step:
            order.append(count - step)
    return order[:count]


def spiral_at(s, count):
    half = lax.div(s + 1, 2)
    return jnp.where(lax.rem(s, 2) == 1, half, lax.rem(count - half, count))


def rcopy(src, dst, send_sem, recv_sem, device):
    return pltpu.make_async_remote_copy(
        src_ref=src, dst_ref=dst, send_sem=send_sem, recv_sem=recv_sem,
        device_id=device, device_id_type=MESH)


def tdot(a, b, precision=None):
    return lax.dot_general(a, b, (((0,), (0,)), ((), ())), precision=precision,
                           preferred_element_type=F32)


def coupling_kernel(xs, ys, tile_ref, u_ref, v_ref, om_ref, out_ref,
                    vb0, vb1, ma0, ma1, sa0, sa1, stage, rbuf,
                    own_sem, v_send, v_recv, m_send, m_recv,
                    s_send, f_send, s_recv, r_send, r_recv):
    vb, ma, sa = (vb0, vb1), (ma0, ma1), (sa0, sa1)
    panels = 2
    me = lax.axis_index("rows")
    x, y = lax.div(me, ys), lax.rem(me, ys)
    rows = vb0.shape[1]
    rank = ma0.shape[1]
    listed = tile_ref.shape[1]

    def at(xx, yy):
        return {"rows": lax.rem(xx, xs) * ys + lax.rem(yy, ys)}

    barrier = pltpu.get_barrier_semaphore()
    for dy in range(1, ys):
        pl.semaphore_signal(barrier, inc=1, device_id=at(x, y + dy), device_id_type=MESH)
    for dx in (1, xs - 1):
        pl.semaphore_signal(barrier, inc=1, device_id=at(x + dx, y), device_id_type=MESH)

    own = []
    for p in range(panels):
        own.append(pltpu.make_async_copy(
            v_ref.at[p, pl.ds(pl.multiple_of(y * rows, rows), rows), :],
            vb[p].at[y], own_sem.at[p]))
        own[p].start()
    pl.semaphore_wait(barrier, ys + 1)

    def send_v(p):
        def body(s, carry):
            yd = lax.rem(y + spiral_at(s, ys), ys)
            rcopy(v_ref.at[p, pl.ds(pl.multiple_of(yd * rows, rows), rows), :],
                  vb[p].at[y], v_send.at[p, s], v_recv.at[p, y], at(x, yd)).start()
            return carry
        lax.fori_loop(1, ys, body, 0)

    def send_m(p):
        ma[p][y] = tdot(u_ref[p], om_ref[...]).astype(BF16)

        def body(s, carry):
            yd = lax.rem(y + spiral_at(s, ys), ys)
            rcopy(ma[p].at[y], ma[p].at[y], m_send.at[p, s], m_recv.at[p, y],
                  at(x, yd)).start()
            return carry
        lax.fori_loop(1, ys, body, 0)

    def wait_in(ref, sem):
        rcopy(ref, ref, sem, sem, at(x, y)).wait_recv()

    def wait_out(ref, sem):
        rcopy(ref, ref, sem, sem, at(x, y)).wait_send()

    def sketch_block(p, yd):
        block = x * ys + yd
        sa[p][block] = jnp.dot(vb[p][yd], ma[p][yd], preferred_element_type=F32).astype(BF16)
        for side, dx in enumerate((1, xs - 1)):
            rcopy(sa[p].at[block], sa[p].at[block], s_send.at[p, side, yd],
                  s_recv.at[p, block], at(x + dx, y)).start()

    def forward(p, yd):
        come, go = ((xs - 1, 1), (1, xs - 1))[p]
        block = lax.rem(x + come, xs) * ys + yd
        wait_in(sa[p].at[block], s_recv.at[p, block])
        rcopy(sa[p].at[block], sa[p].at[block], f_send.at[p, yd],
              s_recv.at[p, block], at(x + go, y)).start()

    def sketch_panel(p):
        own[p].wait()
        sketch_block(p, y)

        def body(s, carry):
            yd = lax.rem(y + spiral_at(s, ys), ys)
            wait_in(vb[p].at[yd], v_recv.at[p, yd])
            wait_in(ma[p].at[yd], m_recv.at[p, yd])
            sketch_block(p, yd)
            forward(p, lax.rem(y + spiral_at(s - 1, ys), ys))
            return carry
        lax.fori_loop(1, ys, body, 0)
        forward(p, lax.rem(y + spiral_at(ys - 1, ys), ys))

    def rest_in(p):
        def body(yd, carry):
            for dx in ((1, 2), (2, xs - 1))[p]:
                block = lax.rem(x + dx, xs) * ys + yd
                wait_in(sa[p].at[block], s_recv.at[p, block])
            return carry
        lax.fori_loop(0, ys, body, 0)

    def part(p, yd):
        row = x * ys + yd
        picked = jnp.concatenate([sa[p][tile_ref[row, t]] for t in range(listed)], axis=1)
        return tdot(vb[p][yd], picked)

    chain = ((ys // 2, ys - 1 - ys // 2), (ys - 1 - ys // 2, ys // 2))

    def ring_step(p, s):
        for side in range(2):
            length = chain[p][side]
            if s >= length:
                continue
            away = length - s
            yd = lax.rem(y + (away if side == 0 else ys - away), ys)
            term = part(p, yd)
            if s > 0:
                wait_in(rbuf.at[p, side, s - 1], r_recv.at[p, side, s - 1])
                term = term + rbuf[p, side, s - 1].astype(F32)
            stage[p, side, s] = term.astype(BF16)
            rcopy(stage.at[p, side, s], rbuf.at[p, side, s], r_send.at[p, side, s],
                  r_recv.at[p, side, s], at(x, y + (1 if side == 0 else ys - 1))).start()

    def ring_end(p):
        term = part(p, y)
        for side in range(2):
            last = chain[p][side] - 1
            wait_in(rbuf.at[p, side, last], r_recv.at[p, side, last])
            term = term + rbuf[p, side, last].astype(F32)
        out_ref[p * rank:(p + 1) * rank, :] = term.astype(BF16)

    send_v(0)
    send_m(0)
    send_m(1)
    send_v(1)
    sketch_panel(0)
    sketch_panel(1)
    for p in range(panels):
        rest_in(p)
        for s in range(ys // 2):
            ring_step(p, s)
        ring_end(p)

    for p in range(panels):
        def drain(s, carry):
            wait_out(vb[p].at[y], v_send.at[p, s])
            wait_out(ma[p].at[y], m_send.at[p, s])
            return carry
        lax.fori_loop(1, ys, drain, 0)

        def drain_s(yd, carry):
            for side in range(2):
                wait_out(sa[p].at[yd], s_send.at[p, side, yd])
            wait_out(sa[p].at[yd], f_send.at[p, yd])
            return carry
        lax.fori_loop(0, ys, drain_s, 0)
        for side in range(2):
            for s in range(chain[p][side]):
                wait_out(stage.at[p, side, s], r_send.at[p, side, s])


def sum_kernel(zs, u_ref, c_ref, rows_ref, gram_ref,
               xsend, xrecv, held, stage, rbuf, gpart, gx, ghalf, gr, gsum, gall, gout,
               x_send, x_recv, r_send, r_recv, g_send, g_recv,
               a_send, a_recv, b_send, b_recv, e_send, e_recv):
    me = lax.axis_index("depth")
    z, c = lax.div(me, CORES), lax.rem(me, CORES)
    rows, width = rows_ref.shape
    half = width // 2
    rank = gram_ref.shape[1]
    tiles = width // rank
    panels = u_ref.shape[0]

    def at(zz, cc):
        return {"depth": lax.rem(zz, zs) * CORES + cc}

    def wait_in(ref, sem):
        rcopy(ref, ref, sem, sem, at(z, c)).wait_recv()

    def wait_out(ref, sem):
        rcopy(ref, ref, sem, sem, at(z, c)).wait_send()

    barrier = pltpu.get_barrier_semaphore()
    for dz in range(1, zs):
        pl.semaphore_signal(barrier, inc=1, device_id=at(z + dz, c), device_id_type=MESH)
    pl.semaphore_signal(barrier, inc=1, device_id=at(z, 1 - c), device_id_type=MESH)

    def block(zd, cd):
        start = pl.multiple_of((zd * CORES + cd) * rows, rows)
        left = jnp.concatenate([u_ref[p, pl.ds(start, rows), :] for p in range(panels)], axis=1)
        return jnp.dot(left, c_ref[...], preferred_element_type=F32)

    chain = ((zs // 2, zs - 1 - zs // 2), (zs - 1 - zs // 2, zs // 2))
    far_first = [zs // 2]
    for away in range(zs // 2 - 1, 0, -1):
        far_first += [away, zs - away]
    far_first.append(0)

    pl.semaphore_wait(barrier, zs)
    for away in far_first:
        zd = lax.rem(z + away, zs)
        xsend[zd] = block(zd, 1 - c)
        rcopy(xsend.at[zd], xrecv.at[zd], x_send.at[zd], x_recv.at[zd], at(z, 1 - c)).start()
    for away in far_first:
        zd = lax.rem(z + away, zs)
        mine = block(zd, c)
        wait_in(xrecv.at[zd], x_recv.at[zd])
        held[zd] = mine + xrecv[zd]

    for s in range(zs // 2):
        for h in range(2):
            for side in range(2):
                length = chain[h][side]
                if s >= length:
                    continue
                away = length - s
                zd = lax.rem(z + (away if side == 0 else zs - away), zs)
                term = held[zd, :, h * half:(h + 1) * half]
                if s > 0:
                    wait_in(rbuf.at[h, side, s - 1], r_recv.at[h, side, s - 1])
                    term = term + rbuf[h, side, s - 1].astype(F32)
                stage[h, side, s] = term.astype(BF16)
                rcopy(stage.at[h, side, s], rbuf.at[h, side, s], r_send.at[h, side, s],
                      r_recv.at[h, side, s], at(z + (1 if side == 0 else zs - 1), c)).start()
    for h in range(2):
        term = held[z, :, h * half:(h + 1) * half]
        for side in range(2):
            last = chain[h][side] - 1
            wait_in(rbuf.at[h, side, last], r_recv.at[h, side, last])
            term = term + rbuf[h, side, last].astype(F32)
        rows_ref[:, h * half:(h + 1) * half] = term

    for t in range(tiles):
        own = rows_ref[:, t * rank:(t + 1) * rank]
        gpart[t * rank:(t + 1) * rank, :] = tdot(own, own, HIGHEST)
    size = tiles * rank // CORES
    piece = size // zs
    theirs = pl.ds(pl.multiple_of((1 - c) * size, size), size)
    mine = pl.ds(pl.multiple_of(c * size, size), size)
    rcopy(gpart.at[theirs, :], gx, g_send, g_recv, at(z, 1 - c)).start()
    wait_in(gx, g_recv)
    ghalf[...] = gpart[mine, :] + gx[...]

    def piece_of(zd):
        return pl.ds(pl.multiple_of(zd * piece, piece), piece)

    for dz in range(1, zs):
        zd = lax.rem(z + dz, zs)
        rcopy(ghalf.at[piece_of(zd), :], gr.at[z], a_send.at[zd], a_recv.at[z], at(zd, c)).start()
    gr[z] = ghalf[piece_of(z), :]
    for dz in range(1, zs):
        zd = lax.rem(z + dz, zs)
        wait_in(gr.at[zd], a_recv.at[zd])
    total = gr[0]
    for k in range(1, zs):
        total = total + gr[k]
    gall[piece_of(z), :] = total
    for dz in range(1, zs):
        zd = lax.rem(z + dz, zs)
        rcopy(gall.at[piece_of(z), :], gall.at[piece_of(z), :], b_send.at[zd], b_recv.at[z],
              at(zd, c)).start()
    for dz in range(1, zs):
        zd = lax.rem(z + dz, zs)
        wait_in(gall.at[piece_of(zd), :], b_recv.at[zd])
    rcopy(gall, gout, e_send, e_recv, at(z, 1 - c)).start()
    gram_ref[mine, :] = gall[...]
    wait_in(gout, e_recv)
    gram_ref[theirs, :] = gout[...]

    for zd in range(zs):
        wait_out(xsend.at[zd], x_send.at[zd])
    for h in range(2):
        for side in range(2):
            for s in range(chain[h][side]):
                wait_out(stage.at[h, side, s], r_send.at[h, side, s])
    wait_out(gx, g_send)
    for dz in range(1, zs):
        zd = lax.rem(z + dz, zs)
        wait_out(gr.at[zd], a_send.at[zd])
        wait_out(gr.at[zd], b_send.at[zd])
    wait_out(gall, e_send)


def factor_kernel(scale, rows_ref, gram_ref, basis_ref, chol_ref):
    rank = gram_ref.shape[1]
    tiles = gram_ref.shape[0] // rank
    size = 128 // tiles
    lane = lax.broadcasted_iota(jnp.int32, (size, 128), 1)
    sub = lax.broadcasted_iota(jnp.int32, (size, 128), 0)
    first = (lane // size) * size
    unit = (lane - first == sub).astype(F32)

    def dott(a, b):
        return lax.dot_general(a, b, (((1,), (1,)), ((), ())), precision=HIGHEST,
                               preferred_element_type=F32)

    def dot(a, b):
        return jnp.dot(a, b, precision=HIGHEST, preferred_element_type=F32)

    trail = [gram_ref[t * rank:(t + 1) * rank, :] for t in range(tiles)]
    eye = (lax.broadcasted_iota(jnp.int32, (rank, rank), 0)
           == lax.broadcasted_iota(jnp.int32, (rank, rank), 1)).astype(F32)
    rest_inv = [eye] * tiles
    done = [[] for _ in range(tiles)]
    for b in range(rank // size):
        packed = jnp.concatenate([trail[t][:size, :size] for t in range(tiles)], axis=1)
        inv = unit
        pivots = jnp.ones((size, 128), F32)
        for k in range(size):
            column = jnp.take_along_axis(packed, first + k, axis=1)
            pivot = column[k:k + 1, :]
            times = jnp.where(sub > k, column / pivot, 0.0)
            pivots = jnp.where(sub == k, pivot, pivots)
            packed = packed - times * packed[k:k + 1, :]
            inv = inv - times * inv[k:k + 1, :]
        inv = inv * lax.rsqrt(pivots)
        for t in range(tiles):
            small = inv[:, t * size:(t + 1) * size]
            head = dot(small, rest_inv[t][:size, :])
            done[t].append(head)
            if (b + 1) * size < rank:
                below = dott(trail[t][size:, :size], small)
                trail[t] = trail[t][size:, size:] - dott(below, below)
                rest_inv[t] = rest_inv[t][size:, :] - dot(below, head)
    row = lax.broadcasted_iota(jnp.int32, (rank, rank), 0)
    col = lax.broadcasted_iota(jnp.int32, (rank, rank), 1)
    for t in range(tiles):
        inverse = jnp.concatenate(done[t], axis=0)
        basis_ref[t] = dott(rows_ref[:, t * rank:(t + 1) * rank], inverse) * scale
        lower = dott(gram_ref[t * rank:(t + 1) * rank, :], inverse)
        chol_ref[t] = jnp.where(row >= col, lower * (1.0 / scale), 0.0)


def couplings(tile_list, left, right, probe, xs, ys):
    panels, size, rank = left.shape
    rows = size // ys
    listed = tile_list.shape[1]
    number = xs * ys
    vmem = pl.BlockSpec(memory_space=pltpu.VMEM)
    dma = pltpu.SemaphoreType.DMA
    steps = ys // 2
    return pl.pallas_call(
        functools.partial(coupling_kernel, xs, ys),
        out_shape=jax.ShapeDtypeStruct((panels * rank, listed * rank), BF16),
        in_specs=[pl.BlockSpec(memory_space=pltpu.SMEM), vmem,
                  pl.BlockSpec(memory_space=pl.ANY), vmem],
        out_specs=vmem,
        scratch_shapes=[
            pltpu.VMEM((ys, rows, rank), BF16), pltpu.VMEM((ys, rows, rank), BF16),
            pltpu.VMEM((ys, rank, rank), BF16), pltpu.VMEM((ys, rank, rank), BF16),
            pltpu.VMEM((number, rows, rank), BF16), pltpu.VMEM((number, rows, rank), BF16),
            pltpu.VMEM((panels, 2, steps, rank, listed * rank), BF16),
            pltpu.VMEM((panels, 2, steps, rank, listed * rank), BF16),
            dma((panels,)), dma((panels, ys)), dma((panels, ys)), dma((panels, ys)),
            dma((panels, ys)), dma((panels, 2, ys)), dma((panels, ys)),
            dma((panels, number)), dma((panels, 2, steps)), dma((panels, 2, steps)),
        ],
        compiler_params=pltpu.CompilerParams(
            collective_id=0, has_side_effects=True, vmem_limit_bytes=40 * 2 ** 20),
        name="couplings",
    )(tile_list, left, right, probe)


def sums(left, coupling, zs):
    panels, size, rank = left.shape
    width = coupling.shape[1]
    rows = size // (zs * CORES)
    tiles = width // rank
    vmem = pl.BlockSpec(memory_space=pltpu.VMEM)
    dma = pltpu.SemaphoreType.DMA
    steps = zs // 2
    share = tiles * rank // CORES
    return pl.pallas_call(
        functools.partial(sum_kernel, zs),
        out_shape=(jax.ShapeDtypeStruct((rows, width), F32),
                   jax.ShapeDtypeStruct((tiles * rank, rank), F32)),
        in_specs=[vmem, vmem],
        out_specs=(vmem, vmem),
        scratch_shapes=[
            pltpu.VMEM((zs, rows, width), F32), pltpu.VMEM((zs, rows, width), F32),
            pltpu.VMEM((zs, rows, width), F32),
            pltpu.VMEM((2, 2, steps, rows, width // 2), BF16),
            pltpu.VMEM((2, 2, steps, rows, width // 2), BF16),
            pltpu.VMEM((tiles * rank, rank), F32), pltpu.VMEM((share, rank), F32),
            pltpu.VMEM((share, rank), F32), pltpu.VMEM((zs, share // zs, rank), F32),
            pltpu.VMEM((share // zs, rank), F32),
            pltpu.VMEM((share, rank), F32), pltpu.VMEM((share, rank), F32),
            dma((zs,)), dma((zs,)), dma((2, 2, steps)), dma((2, 2, steps)), dma, dma,
            dma((zs,)), dma((zs,)), dma((zs,)), dma((zs,)), dma, dma,
        ],
        compiler_params=pltpu.CompilerParams(
            collective_id=1, has_side_effects=True, vmem_limit_bytes=40 * 2 ** 20),
        name="sums",
    )(left, coupling)


def factors(rows, gram, scale):
    size, width = rows.shape
    rank = gram.shape[1]
    tiles = width // rank
    vmem = pl.BlockSpec(memory_space=pltpu.VMEM)
    return pl.pallas_call(
        functools.partial(factor_kernel, scale),
        out_shape=(jax.ShapeDtypeStruct((tiles, size, rank), F32),
                   jax.ShapeDtypeStruct((tiles, rank, rank), F32)),
        in_specs=[vmem, vmem],
        out_specs=(vmem, vmem),
        compiler_params=pltpu.CompilerParams(vmem_limit_bytes=40 * 2 ** 20),
        name="factors",
    )(rows, gram)


def solution(mesh):
    rows, depth = mesh.shape["rows"], mesh.shape["depth"]

    def on_device(left_factors, right_factors, probe_matrix, tile_list):
        left, right = left_factors[0], right_factors[0]
        scale = math.sqrt(float(left.shape[1]))
        coupling = couplings(tile_list, left, right, probe_matrix, XS, rows // XS)
        own_rows, gram = sums(left, coupling, depth // CORES)
        basis, lower = factors(own_rows, gram, scale)
        return basis[None], lower[None]

    in_specs = (P("rows", "depth", None, None), P("rows", "depth", None, None), P(), P())
    out_specs = (P("rows", None, "depth", None), P("rows", None, None, None))
    return jax.shard_map(
        on_device, mesh=mesh, in_specs=in_specs, out_specs=out_specs, check_vma=False
    )
```

time: 399 us -> 174 us (0.44)
  Pallas kernels: 0 us -> 169 us
  waiting for transfers between devices: 156 us -> 0 us
  blocking collectives: 101 us -> 0 us
  other arithmetic: 89.8 us -> 0 us
  matrix products: 18.1 us -> 0 us
  between operations: 14.1 us -> 0.67 us
  starting transfers between devices: 10.5 us -> 0 us
  local copies, waits for them, and re-layouts: 9.65 us -> 4.25 us
    pallas_call x0 -> x3, Pallas kernels: none -> 169 us  [the longest x1 90.2 us: couplings(): pl.pallas_call(functools.partial(coupling_kernel, xs, ys), out_shape=jax....]
    psum x1 -> x0, waiting for transfers between devices: 131 us -> none  [on_device(): total = lax.psum(partial_sketch, 'depth')]
    all_to_all x1 -> x0, blocking collectives: 101 us -> none  [on_device(): lax.all_to_all(outgoing, 'rows', split_axis=2, concat_axis=2, tiled=True)]
    another operation x6 -> x0, other arithmetic: 86.4 us -> none  [the longest x4 47.1 us: on_device(): lower = jnp.linalg.cholesky(gram)]
    all_to_all x1 -> x0, waiting for transfers between devices: 24.3 us -> none  [on_device(): lax.all_to_all(sketch_rows[:, None], 'rows', split_axis=2, concat_axis=1,...]
    dot_general x3 -> x0, matrix products: 15.8 us -> none  [the longest x1 7.4 us: on_device(): jnp.einsum('tbk,tbl->tkl', total, total, precision=lax.Precision.HIGHEST)]
    all_to_all x1 -> x0, starting transfers between devices: 10.5 us -> none  [on_device(): lax.all_to_all(sketch_rows[:, None], 'rows', split_axis=2, concat_axis=1,...]
  transfers between devices with their start and end apart: 2 -> 0, of which waited for: 2 -> 0; matrix products, arithmetic and copies ran while one was open for 0% -> 0% of each run, Pallas kernels for 0% -> 0%
where the time goes in v1:
time: 174 us
  Pallas kernels  169 us (97%)
  local copies, waits for them, and re-layouts  4.25 us (2%)
    pallas_call x1, Pallas kernels, couplings(): pl.pallas_call(functools.partial(coupling_kernel, xs, ys), out_shape=jax....  90.2 us
    pallas_call x1, Pallas kernels, sums(): pl.pallas_call(functools.partial(sum_kernel, zs), out_shape=(jax.ShapeDty...  61.9 us
    pallas_call x1, Pallas kernels, factors(): pl.pallas_call(functools.partial(factor_kernel, scale), out_shape=(jax.Sh...  16.8 us
    unnamed x11, local copies, waits for them, and re-layouts  4.25 us

profile of v1, /device:TPU:1, one launch (start us, length us, event | category | flops | bytes accessed | tf_op | source)
XLA Modules:
  0.0 173.8 jit_solution(6617324917684605832)
XLA Ops:
  0.6 0.0 copy-start.4
  0.6 0.7 copy-done.4
  1.3 0.1 copy.6.tile_ref
  1.4 0.0 copy-start
  1.4 1.2 copy-done
  2.6 0.0 copy-start.2
  2.6 1.2 copy-done.2
  3.9 0.0 copy-start.3
  3.9 1.0 copy-done.3
  4.9 0.0 copy-start.1
  4.9 90.2 %couplings.1.c_ref = bf16[256,512]{1,0:T(8,128)(2,1)S(1)} custom-call(s32[32,4]{1,0:T(8,128)S(1)} %copy.6.tile_ref, bf16[2,2048,128]{2,1,0:T(8,128)(2,1)S(1)} %bitcast.4, bf16[2,2048,128]{2,1,0:T(8,128)(2,1)S(1)} %bitcast.6, bf16[2048,128]{1,0:T(8,128)(2,1)S(1)} %copy-done.3), custom_call_target="tpu_custom_call" | custom-call | tf_op jit(solution)/shard_map/couplings/pallas_call | solution.py:373
  95.1 0.0 copy-done.1
  95.1 61.9 %sums.1 = (f32[128,512]{1,0:T(8,128)S(1)}, f32[512,128]{1,0:T(8,128)S(1)}) custom-call(bf16[2,2048,128]{2,1,0:T(8,128)(2,1)S(1)} %bitcast.5, bf16[256,512]{1,0:T(8,128)(2,1)S(1)} %couplings.1.c_ref), custom_call_target="tpu_custom_call" | custom-call | tf_op jit(solution)/shard_map/sums/pallas_call | solution.py:404
  157.0 16.8 %factors.1 = (f32[4,128,128]{2,1,0:T(8,128)}, f32[4,128,128]{2,1,0:T(8,128)}) custom-call(f32[128,512]{1,0:T(8,128)S(1)} %get-tuple-element.6.rows_ref, f32[512,128]{1,0:T(8,128)S(1)} %get-tuple-element.7.gram_ref), custom_call_target="tpu_custom_call" | custom-call | tf_op jit(solution)/shard_map/factors/pallas_call | solution.py:433
Async XLA Ops:
  0.6 0.7 copy-start.4
  1.4 1.2 copy-start
  2.6 1.2 copy-start.2
  3.9 1.0 copy-start.3
  4.9 90.2 %copy-start.1 = (bf16[1,2,2048,128]{3,2,1,0:T(8,128)(2,1)S(1)}, bf16[1,2,2048,128]{3,2,1,0:T(8,128)(2,1)}, u32[]{:S(2)}) copy-start(bf16[1,2,2048,128]{3,2,1,0:T(8,128)(2,1)} %param.4) | copy-start | bytes 3145732

commit v2 on v0

v2 whole, which is shorter than its diff:
```python
import functools
import math

import jax
import jax.numpy as jnp
from jax import lax
from jax.experimental import pallas as pl
from jax.experimental.pallas import tpu as pltpu
from jax.sharding import PartitionSpec as P

MESH = pl.DeviceIdType.MESH
F32 = jnp.float32
BF16 = jnp.bfloat16
XS = 4
CORES = 2
HIGHEST = lax.Precision.HIGHEST


def rcopy(src, dst, send_sem, recv_sem, device):
    return pltpu.make_async_remote_copy(
        src_ref=src, dst_ref=dst, send_sem=send_sem, recv_sem=recv_sem,
        device_id=device, device_id_type=MESH)


def tdot(a, b, precision=None):
    return lax.dot_general(a, b, (((0,), (0,)), ((), ())), precision=precision,
                           preferred_element_type=F32)


def update_kernel(xs, ys, zs, tile_ref, u_ref, v_ref, om_ref, rows_ref, gram_ref,
                  uv, om, vb0, vb1, ma, sa0, sa1, stage, rbuf, cpl,
                  xsend, xrecv, held, zstage, zbuf, gpart, gx, ghalf, gr, gall, gout,
                  u_sem, om_sem, own_sem, v_send, v_recv, m_send, m_recv,
                  s_send, f_send, s_recv, r_send, r_recv, x_send, x_recv,
                  z_send, z_recv, g_send, g_recv, a_send, a_recv, b_send, b_recv,
                  e_send, e_recv):
    vb, sa = (vb0, vb1), (sa0, sa1)
    panels, halves = 2, 2
    me, deep = lax.axis_index("rows"), lax.axis_index("depth")
    x, y = lax.div(me, ys), lax.rem(me, ys)
    z, c = lax.div(deep, CORES), lax.rem(deep, CORES)
    rows = vb0.shape[1]
    rank = ma.shape[2]
    listed = tile_ref.shape[1]
    per_half = listed // halves
    width = per_half * rank
    own_rows = rows_ref.shape[0]

    def at_x(dx):
        return {"rows": lax.rem(x + dx + xs, xs) * ys + y}

    def at_y(dy):
        return {"rows": x * ys + lax.rem(y + dy + ys, ys)}

    def at_z(dz):
        return {"depth": lax.rem(z + dz + zs, zs) * CORES + c}

    partner = {"depth": z * CORES + 1 - c}

    def wait_in(ref, sem):
        rcopy(ref, ref, sem, sem, partner).wait_recv()

    def wait_out(ref, sem):
        rcopy(ref, ref, sem, sem, partner).wait_send()

    sent = []

    def send(src, dst, send_sem, recv_sem, device):
        rcopy(src, dst, send_sem, recv_sem, device).start()
        sent.append((src, send_sem))

    def yat(dy):
        return lax.rem(y + dy + ys, ys)

    def zat(dz):
        return lax.rem(z + dz + zs, zs)

    u_copies = [pltpu.make_async_copy(u_ref.at[p], uv.at[p], u_sem.at[p]) for p in range(panels)]
    om_copy = pltpu.make_async_copy(om_ref, om, om_sem)
    om_copy.start()
    for copy in u_copies:
        copy.start()

    def v_rows(p, yd):
        return v_ref.at[p, pl.ds(pl.multiple_of(yd * rows, rows), rows), :]

    own = [pltpu.make_async_copy(v_rows(p, y), vb[p].at[y], own_sem.at[p]) for p in range(panels)]
    for copy in own:
        copy.start()
    barrier = pltpu.get_barrier_semaphore()
    greet = ([at_y(dy) for dy in range(1, ys)] + [at_x(1), at_x(-1)]
             + [at_z(dz) for dz in range(1, zs)] + [partner])
    for device in greet:
        pl.semaphore_signal(barrier, inc=1, device_id=device, device_id_type=MESH)
    om_copy.wait()
    for p in range(panels):
        u_copies[p].wait()
        ma[y, p] = tdot(uv[p], om[...]).astype(BF16)
    pl.semaphore_wait(barrier, len(greet))

    m_reach = {1: ys // 2, -1: ys - 1 - ys // 2}

    def send_m(source, go):
        send(ma.at[source], ma.at[source], m_send.at[source, (go + 1) // 2], m_recv.at[source],
             at_y(go))

    near = [0]
    for away in range(1, ys // 2 + 1):
        near += [-away, away] if 2 * away < ys else [-away]

    def sketch_block(p, s):
        yd = yat(near[s])
        if s == 0:
            own[p].wait()
        else:
            wait_in(vb[p].at[yd], v_recv.at[p, yd])
            if p == 0:
                wait_in(ma.at[yd], m_recv.at[yd])
                go = 1 if near[s] < 0 else -1
                if abs(near[s]) < m_reach[go]:
                    send_m(yd, go)
        block = x * ys + yd
        sa[p][block] = jnp.dot(vb[p][yd], ma[yd, p], preferred_element_type=F32).astype(BF16)
        for side, dx in enumerate((1, -1)):
            send(sa[p].at[block], sa[p].at[block], s_send.at[p, side, yd],
                 s_recv.at[p, block], at_x(dx))

    def forward(p, s):
        come, go = ((-1, 1), (1, -1))[p]
        yd = yat(near[s])
        block = lax.rem(x + come + xs, xs) * ys + yd
        wait_in(sa[p].at[block], s_recv.at[p, block])
        send(sa[p].at[block], sa[p].at[block], f_send.at[p, yd], s_recv.at[p, block], at_x(go))

    def rest_in(p):
        for yd in near:
            for dx in ((1, 2), (2, -1))[p]:
                block = lax.rem(x + dx + xs, xs) * ys + yat(yd)
                wait_in(sa[p].at[block], s_recv.at[p, block])

    def part(p, h, yd):
        row = x * ys + yd
        picked = jnp.concatenate(
            [sa[p][tile_ref[row, h * per_half + k]] for k in range(per_half)], axis=1)
        return tdot(vb[p][yd], picked)

    def chain(count, flip, side):
        return count // 2 if (side == 0) != (flip == 1) else count - 1 - count // 2

    def ring_step(p, h, s):
        for side in range(2):
            length = chain(ys, p, side)
            if s >= length:
                continue
            away = length - s
            term = part(p, h, yat(away if side == 0 else -away))
            if s > 0:
                wait_in(rbuf.at[p, h, side, s - 1], r_recv.at[p, h, side, s - 1])
                term = term + rbuf[p, h, side, s - 1].astype(F32)
            stage[p, h, side, s] = term.astype(BF16)
            send(stage.at[p, h, side, s], rbuf.at[p, h, side, s], r_send.at[p, h, side, s],
                 r_recv.at[p, h, side, s], at_y(1 if side == 0 else -1))

    def ring_end(p, h):
        term = part(p, h, y)
        for side in range(2):
            last = chain(ys, p, side) - 1
            wait_in(rbuf.at[p, h, side, last], r_recv.at[p, h, side, last])
            term = term + rbuf[p, h, side, last].astype(F32)
        cpl[h, p * rank:(p + 1) * rank, :] = term.astype(BF16)

    far = [zs // 2]
    for away in range(zs // 2 - 1, 0, -1):
        far += [away, -away]
    far.append(0)

    def term_rows(h, zd, cd):
        start = pl.multiple_of((zd * CORES + cd) * own_rows, own_rows)
        left = jnp.concatenate([uv[p, pl.ds(start, own_rows), :] for p in range(panels)], axis=1)
        return jnp.dot(left, cpl[h], preferred_element_type=F32)

    def give(h):
        for dz in far:
            zd = zat(dz)
            xsend[h, zd] = term_rows(h, zd, 1 - c).astype(BF16)
            send(xsend.at[h, zd], xrecv.at[h, zd], x_send.at[h, zd], x_recv.at[h, zd], partner)

    def take(h, dz):
        zd = zat(dz)
        mine = term_rows(h, zd, c)
        wait_in(xrecv.at[h, zd], x_recv.at[h, zd])
        held[h, zd] = mine + xrecv[h, zd].astype(F32)

    def held_tile(h, k, dz):
        return held[h, zat(dz), :, k * rank:(k + 1) * rank]

    def depth_step(h, s):
        for dz in far:
            if (abs(dz) == zs // 2 - s - 1 and dz != 0) or (s == 0 and abs(dz) == zs // 2):
                take(h, dz)
        for k in range(per_half):
            t = h * per_half + k
            for side in range(2):
                length = chain(zs, k % 2, side)
                if s >= length:
                    continue
                away = length - s
                if away == zs // 2:
                    term = held_tile(h, k, away)
                else:
                    term = held_tile(h, k, away if side == 0 else -away)
                if s > 0:
                    wait_in(zbuf.at[t, side, s - 1], z_recv.at[t, side, s - 1])
                    term = term + zbuf[t, side, s - 1].astype(F32)
                zstage[t, side, s] = term.astype(BF16)
                send(zstage.at[t, side, s], zbuf.at[t, side, s], z_send.at[t, side, s],
                     z_recv.at[t, side, s], at_z(1 if side == 0 else -1))

    def depth_end(h):
        take(h, 0)
        for k in range(per_half):
            t = h * per_half + k
            term = held_tile(h, k, 0)
            for side in range(2):
                last = chain(zs, k % 2, side) - 1
                wait_in(zbuf.at[t, side, last], z_recv.at[t, side, last])
                term = term + zbuf[t, side, last].astype(F32)
            rows_ref[:, t * rank:(t + 1) * rank] = term
            gpart[t] = tdot(term, term, HIGHEST)

    piece = rank // zs

    def piece_of(zd):
        return pl.ds(pl.multiple_of(zd * piece, piece), piece)

    def gram_swap(h):
        send(gpart.at[h * CORES + 1 - c], gx.at[h], g_send.at[h], g_recv.at[h], partner)

    def gram_spread(h):
        wait_in(gx.at[h], g_recv.at[h])
        ghalf[h] = gpart[h * CORES + c] + gx[h]
        for dz in near_z:
            send(ghalf.at[h, piece_of(zat(dz)), :], gr.at[h, z], a_send.at[h, zat(dz)],
                 a_recv.at[h, z], at_z(dz))
        gr[h, z] = ghalf[h, piece_of(z), :]

    def gram_gather(h):
        for dz in near_z:
            wait_in(gr.at[h, zat(dz)], a_recv.at[h, zat(dz)])
        total = gr[h, 0]
        for k in range(1, zs):
            total = total + gr[h, k]
        gall[h, piece_of(z), :] = total
        for dz in near_z:
            send(gall.at[h, piece_of(z), :], gall.at[h, piece_of(z), :], b_send.at[h, zat(dz)],
                 b_recv.at[h, z], at_z(dz))

    def gram_back(h):
        for dz in near_z:
            wait_in(gall.at[h, piece_of(zat(dz)), :], b_recv.at[h, zat(dz)])
        send(gall.at[h], gout.at[h], e_send.at[h], e_recv.at[h], partner)
        gram_ref[h * CORES + c] = gall[h]

    def gram_end(h):
        wait_in(gout.at[h], e_recv.at[h])
        gram_ref[h * CORES + 1 - c] = gout[h]

    near_z = [dz for dz in reversed(far) if dz != 0]

    turns = [(0, 0), (1, 0)]
    for s in range(1, ys, 2):
        turns += [(p, k) for p in range(panels) for k in (s, s + 1) if k < ys]
    queue = [(p, near[s]) for p, s in turns if s > 0]

    def send_next():
        if queue:
            p, dy = queue.pop(0)
            send(v_rows(p, yat(dy)), vb[p].at[y], v_send.at[p, yat(dy)], v_recv.at[p, y], at_y(dy))

    send_m(y, 1)
    send_m(y, -1)
    for _ in range(4):
        send_next()
    late = []
    for turn in turns:
        sketch_block(*turn)
        if turn[1] > 0:
            send_next()
        late.append(turn)
        if len(late) > 4:
            forward(*late.pop(0))
    for turn in late:
        forward(*turn)
    for p in range(panels):
        rest_in(p)
    for s in range(ys // 2):
        for p in range(panels):
            for h in range(halves):
                ring_step(p, h, s)
    for h in range(halves):
        for p in range(panels):
            ring_end(p, h)
        give(h)
    for s in range(zs // 2):
        for h in range(halves):
            depth_step(h, s)
    for stepper in (depth_end, gram_swap, gram_spread, gram_gather, gram_back, gram_end):
        for h in range(halves):
            stepper(h)
    for ref, sem in sent:
        wait_out(ref, sem)


def factor_kernel(scale, rows_ref, gram_ref, basis_ref, chol_ref):
    rank = gram_ref.shape[1]
    tiles = gram_ref.shape[0] // rank
    size = 128 // tiles
    lane = lax.broadcasted_iota(jnp.int32, (size, 128), 1)
    sub = lax.broadcasted_iota(jnp.int32, (size, 128), 0)
    first = (lane // size) * size
    unit = (lane - first == sub).astype(F32)

    def dott(a, b):
        return lax.dot_general(a, b, (((1,), (1,)), ((), ())), precision=HIGHEST,
                               preferred_element_type=F32)

    def dot(a, b):
        return jnp.dot(a, b, precision=HIGHEST, preferred_element_type=F32)

    trail = [gram_ref[t * rank:(t + 1) * rank, :] for t in range(tiles)]
    eye = (lax.broadcasted_iota(jnp.int32, (rank, rank), 0)
           == lax.broadcasted_iota(jnp.int32, (rank, rank), 1)).astype(F32)
    rest_inv = [eye] * tiles
    done = [[] for _ in range(tiles)]
    for b in range(rank // size):
        packed = jnp.concatenate([trail[t][:size, :size] for t in range(tiles)], axis=1)
        inv = unit
        pivots = jnp.ones((size, 128), F32)
        for k in range(size):
            column = jnp.take_along_axis(packed, first + k, axis=1)
            pivot = column[k:k + 1, :]
            times = jnp.where(sub > k, column / pivot, 0.0)
            pivots = jnp.where(sub == k, pivot, pivots)
            packed = packed - times * packed[k:k + 1, :]
            inv = inv - times * inv[k:k + 1, :]
        inv = inv * lax.rsqrt(pivots)
        for t in range(tiles):
            small = inv[:, t * size:(t + 1) * size]
            head = dot(small, rest_inv[t][:size, :])
            done[t].append(head)
            if (b + 1) * size < rank:
                below = dott(trail[t][size:, :size], small)
                trail[t] = trail[t][size:, size:] - dott(below, below)
                rest_inv[t] = rest_inv[t][size:, :] - dot(below, head)
    row = lax.broadcasted_iota(jnp.int32, (rank, rank), 0)
    col = lax.broadcasted_iota(jnp.int32, (rank, rank), 1)
    for t in range(tiles):
        inverse = jnp.concatenate(done[t], axis=0)
        basis_ref[t] = dott(rows_ref[:, t * rank:(t + 1) * rank], inverse) * scale
        lower = dott(gram_ref[t * rank:(t + 1) * rank, :], inverse)
        chol_ref[t] = jnp.where(row >= col, lower * (1.0 / scale), 0.0)


def updates(tile_list, left, right, probe, xs, ys, zs):
    panels, size, rank = left.shape
    rows, own_rows = size // ys, size // (zs * CORES)
    listed = tile_list.shape[1]
    number = xs * ys
    width = listed * rank // 2
    vmem = pl.BlockSpec(memory_space=pltpu.VMEM)
    hbm = pl.BlockSpec(memory_space=pl.ANY)
    dma = pltpu.SemaphoreType.DMA
    ysteps, zsteps = ys // 2, zs // 2
    return pl.pallas_call(
        functools.partial(update_kernel, xs, ys, zs),
        out_shape=(jax.ShapeDtypeStruct((own_rows, listed * rank), F32),
                   jax.ShapeDtypeStruct((listed, rank, rank), F32)),
        in_specs=[pl.BlockSpec(memory_space=pltpu.SMEM), hbm, hbm, hbm],
        out_specs=(vmem, vmem),
        scratch_shapes=[
            pltpu.VMEM((panels, size, rank), BF16), pltpu.VMEM((size, rank), BF16),
            pltpu.VMEM((ys, rows, rank), BF16), pltpu.VMEM((ys, rows, rank), BF16),
            pltpu.VMEM((ys, panels, rank, rank), BF16),
            pltpu.VMEM((number, rows, rank), BF16), pltpu.VMEM((number, rows, rank), BF16),
            pltpu.VMEM((panels, 2, 2, ysteps, rank, width), BF16),
            pltpu.VMEM((panels, 2, 2, ysteps, rank, width), BF16),
            pltpu.VMEM((2, panels * rank, width), BF16),
            pltpu.VMEM((2, zs, own_rows, width), BF16), pltpu.VMEM((2, zs, own_rows, width), BF16),
            pltpu.VMEM((2, zs, own_rows, width), F32),
            pltpu.VMEM((listed, 2, zsteps, own_rows, rank), BF16),
            pltpu.VMEM((listed, 2, zsteps, own_rows, rank), BF16),
            pltpu.VMEM((listed, rank, rank), F32), pltpu.VMEM((2, rank, rank), F32),
            pltpu.VMEM((2, rank, rank), F32), pltpu.VMEM((2, zs, rank // zs, rank), F32),
            pltpu.VMEM((2, rank, rank), F32), pltpu.VMEM((2, rank, rank), F32),
            dma((panels,)), dma, dma((panels,)), dma((panels, ys)), dma((panels, ys)),
            dma((ys, 2)), dma((ys,)), dma((panels, 2, ys)), dma((panels, ys)),
            dma((panels, number)), dma((panels, 2, 2, ysteps)), dma((panels, 2, 2, ysteps)),
            dma((2, zs)), dma((2, zs)), dma((listed, 2, zsteps)), dma((listed, 2, zsteps)),
            dma((2,)), dma((2,)), dma((2, zs)), dma((2, zs)), dma((2, zs)), dma((2, zs)),
            dma((2,)), dma((2,)),
        ],
        compiler_params=pltpu.CompilerParams(
            collective_id=0, has_side_effects=True, vmem_limit_bytes=56 * 2 ** 20),
        name="updates",
    )(tile_list, left, right, probe)


def factors(rows, gram, scale):
    size, width = rows.shape
    rank = gram.shape[1]
    tiles = width // rank
    vmem = pl.BlockSpec(memory_space=pltpu.VMEM)
    return pl.pallas_call(
        functools.partial(factor_kernel, scale),
        out_shape=(jax.ShapeDtypeStruct((tiles, size, rank), F32),
                   jax.ShapeDtypeStruct((tiles, rank, rank), F32)),
        in_specs=[vmem, vmem],
        out_specs=(vmem, vmem),
        compiler_params=pltpu.CompilerParams(vmem_limit_bytes=40 * 2 ** 20),
        name="factors",
    )(rows, gram)


def solution(mesh):
    rows, depth = mesh.shape["rows"], mesh.shape["depth"]

    def on_device(left_factors, right_factors, probe_matrix, tile_list):
        left, right = left_factors[0], right_factors[0]
        scale = math.sqrt(float(left.shape[1]))
        own_rows, gram = updates(tile_list, left, right, probe_matrix,
                                 XS, rows // XS, depth // CORES)
        gram = gram.reshape(-1, gram.shape[2])
        basis, lower = factors(own_rows, gram, scale)
        return basis[None], lower[None]

    in_specs = (P("rows", "depth", None, None), P("rows", "depth", None, None), P(), P())
    out_specs = (P("rows", None, "depth", None), P("rows", None, None, None))
    return jax.shard_map(
        on_device, mesh=mesh, in_specs=in_specs, out_specs=out_specs, check_vma=False
    )
```

time: 399 us -> 133 us (0.33)
  waiting for transfers between devices: 156 us -> 0 us
  Pallas kernels: 0 us -> 129 us
  blocking collectives: 101 us -> 0 us
  other arithmetic: 89.8 us -> 0 us
  matrix products: 18.1 us -> 0 us
  between operations: 14.1 us -> 0.66 us
  starting transfers between devices: 10.5 us -> 0 us
  local copies, waits for them, and re-layouts: 9.65 us -> 3.26 us
    psum x1 -> x0, waiting for transfers between devices: 131 us -> none  [on_device(): total = lax.psum(partial_sketch, 'depth')]
    pallas_call x0 -> x2, Pallas kernels: none -> 129 us  [the longest x1 112 us: updates(): pl.pallas_call(functools.partial(update_kernel, xs, ys, zs), out_shape=(j...]
    all_to_all x1 -> x0, blocking collectives: 101 us -> none  [on_device(): lax.all_to_all(outgoing, 'rows', split_axis=2, concat_axis=2, tiled=True)]
    another operation x6 -> x0, other arithmetic: 86.4 us -> none  [the longest x4 47.1 us: on_device(): lower = jnp.linalg.cholesky(gram)]
    all_to_all x1 -> x0, waiting for transfers between devices: 24.3 us -> none  [on_device(): lax.all_to_all(sketch_rows[:, None], 'rows', split_axis=2, concat_axis=1,...]
    dot_general x3 -> x0, matrix products: 15.8 us -> none  [the longest x1 7.4 us: on_device(): jnp.einsum('tbk,tbl->tkl', total, total, precision=lax.Precision.HIGHEST)]
    all_to_all x1 -> x0, starting transfers between devices: 10.5 us -> none  [on_device(): lax.all_to_all(sketch_rows[:, None], 'rows', split_axis=2, concat_axis=1,...]
  transfers between devices with their start and end apart: 2 -> 0, of which waited for: 2 -> 0; matrix products, arithmetic and copies ran while one was open for 0% -> 0% of each run, Pallas kernels for 0% -> 0%
where the time goes in v2:
time: 133 us
  Pallas kernels  129 us (97%)
  local copies, waits for them, and re-layouts  3.26 us (2%)
    pallas_call x1, Pallas kernels, updates(): pl.pallas_call(functools.partial(update_kernel, xs, ys, zs), out_shape=(j...  112 us
    pallas_call x1, Pallas kernels, factors(): pl.pallas_call(functools.partial(factor_kernel, scale), out_shape=(jax.Sh...  16.8 us
    unnamed x7, local copies, waits for them, and re-layouts  3.26 us

profile of v2, /device:TPU:1, one launch (start us, length us, event | category | flops | bytes accessed | tf_op | source)
XLA Modules:
  0.0 132.5 jit_solution(2995060316033441513)
XLA Ops:
  0.6 0.0 copy-start.2
  0.6 0.7 copy-done.2
  1.3 0.7 copy.6.tile_ref
  2.0 111.8 %updates.1 = (f32[128,512]{1,0:T(8,128)}, f32[4,128,128]{2,1,0:T(8,128)}) custom-call(s32[32,4]{1,0:T(8,128)} %copy.6.tile_ref, bf16[2,2048,128]{2,1,0:T(8,128)(2,1)} %bitcast.6, bf16[2,2048,128]{2,1,0:T(8,128)(2,1)} %bitcast.7, bf16[2048,128]{1,0:T(8,128)(2,1)} %om_ref.1), custom_call_target="tpu_custom_call" | custom-call | tf_op jit(solution)/shard_map/updates/pallas_call | solution.py:374
  113.8 0.0 copy-start
  113.8 0.9 copy-done
  114.7 0.0 copy-start.1
  114.8 0.9 copy-done.1
  115.7 16.8 %factors.1 = (f32[4,128,128]{2,1,0:T(8,128)}, f32[4,128,128]{2,1,0:T(8,128)}) custom-call(f32[128,512]{1,0:T(8,128)S(1)} %copy-done, f32[512,128]{1,0:T(8,128)S(1)} %bitcast.5), custom_call_target="tpu_custom_call" | custom-call | tf_op jit(solution)/shard_map/factors/pallas_call | solution.py:413
Async XLA Ops:
  0.6 0.7 copy-start.2
  113.8 1.0 copy-start
  114.7 0.9 copy-start.1

commit v3 on v2

--- a/solution.py
+++ b/solution.py
@@ -27,13 +27,13 @@
                            preferred_element_type=F32)
 
 
-def update_kernel(xs, ys, zs, tile_ref, u_ref, v_ref, om_ref, rows_ref, gram_ref,
-                  uv, om, vb0, vb1, ma, sa0, sa1, stage, rbuf, cpl,
+def update_kernel(xs, ys, zs, tile_ref, u_ref, v_ref, om_ref, rows_out, gram_out,
+                  rows_ref, uv, om, vb0, vb1, ma, sa0, sa1, stage, rbuf, cpl,
                   xsend, xrecv, held, zstage, zbuf, gpart, gx, ghalf, gr, gall, gout,
                   u_sem, om_sem, own_sem, v_send, v_recv, m_send, m_recv,
                   s_send, f_send, s_recv, r_send, r_recv, x_send, x_recv,
                   z_send, z_recv, g_send, g_recv, a_send, a_recv, b_send, b_recv,
-                  e_send, e_recv):
+                  e_send, e_recv, rows_sem, tile_sem):
     vb, sa = (vb0, vb1), (sa0, sa1)
     panels, halves = 2, 2
     me, deep = lax.axis_index("rows"), lax.axis_index("depth")
@@ -41,7 +41,7 @@
     z, c = lax.div(deep, CORES), lax.rem(deep, CORES)
     rows = vb0.shape[1]
     rank = ma.shape[2]
-    listed = tile_ref.shape[1]
+    listed = tile_ref.shape[0]
     per_half = listed // halves
     width = per_half * rank
     own_rows = rows_ref.shape[0]
@@ -141,7 +141,7 @@
     def part(p, h, yd):
         row = x * ys + yd
         picked = jnp.concatenate(
-            [sa[p][tile_ref[row, h * per_half + k]] for k in range(per_half)], axis=1)
+            [sa[p][tile_ref[h * per_half + k, row]] for k in range(per_half)], axis=1)
         return tdot(vb[p][yd], picked)
 
     def chain(count, flip, side):
@@ -233,6 +233,12 @@
     def piece_of(zd):
         return pl.ds(pl.multiple_of(zd * piece, piece), piece)
 
+    rows_copy = pltpu.make_async_copy(rows_ref, rows_out, rows_sem)
+
+    def tile_copy(ref, h, core):
+        tile = h * CORES + core
+        return pltpu.make_async_copy(ref.at[h], gram_out.at[tile], tile_sem.at[tile])
+
     def gram_swap(h):
         send(gpart.at[h * CORES + 1 - c], gx.at[h], g_send.at[h], g_recv.at[h], partner)
 
@@ -259,11 +265,11 @@
         for dz in near_z:
             wait_in(gall.at[h, piece_of(zat(dz)), :], b_recv.at[h, zat(dz)])
         send(gall.at[h], gout.at[h], e_send.at[h], e_recv.at[h], partner)
-        gram_ref[h * CORES + c] = gall[h]
+        tile_copy(gall, h, c).start()
 
     def gram_end(h):
         wait_in(gout.at[h], e_recv.at[h])
-        gram_ref[h * CORES + 1 - c] = gout[h]
+        tile_copy(gout, h, 1 - c).start()
 
     near_z = [dz for dz in reversed(far) if dz != 0]
 
@@ -287,38 +293,89 @@
         if turn[1] > 0:
             send_next()
         late.append(turn)
-        if len(late) > 4:
+        if len(late) > 3:
             forward(*late.pop(0))
     for turn in late:
         forward(*turn)
     for p in range(panels):
         rest_in(p)
     for s in range(ys // 2):
-        for p in range(panels):
-            for h in range(halves):
+        for h in range(halves):
+            for p in range(panels):
                 ring_step(p, h, s)
     for h in range(halves):
         for p in range(panels):
             ring_end(p, h)
         give(h)
-    for s in range(zs // 2):
+        depth_step(h, 0)
+    for s in range(1, zs // 2):
         for h in range(halves):
             depth_step(h, s)
-    for stepper in (depth_end, gram_swap, gram_spread, gram_gather, gram_back, gram_end):
+    for h in range(halves):
+        depth_end(h)
+        gram_swap(h)
+    rows_copy.start()
+    for stepper in (gram_spread, gram_gather, gram_back, gram_end):
         for h in range(halves):
             stepper(h)
     for ref, sem in sent:
         wait_out(ref, sem)
-
-
-def factor_kernel(scale, rows_ref, gram_ref, basis_ref, chol_ref):
+    rows_copy.wait()
+    for h in range(halves):
+        tile_copy(gall, h, c).wait()
+        tile_copy(gout, h, 1 - c).wait()
+
+
+def eliminate(packed, size, wide):
+    groups = size // 8
+    sub = lax.broadcasted_iota(jnp.int32, (8, 128), 0)
+    lane = lax.broadcasted_iota(jnp.int32, (8, 128), 1)
+    head = (lane // size) * size
+    left = [packed[8 * g:8 * g + 8, :] for g in range(groups)]
+    inv = [(lane - head == sub + 8 * g).astype(F32) for g in range(groups)]
+    scales = [None] * groups
+
+    def spread(array, row):
+        return jnp.broadcast_to(array[row:row + 1, :], (8, 128))
+
+    for start in range(0, size, wide):
+        top, row = start // 8, start % 8
+        columns = [[jnp.take_along_axis(left[g], head + (start + j), axis=1)
+                    for g in range(top, groups)] for j in range(wide)]
+        small = [[spread(columns[j][0], row + i) for j in range(i + 1)] for i in range(wide)]
+        pivot_rows = [spread(left[top], row + j) for j in range(wide)]
+        inv_rows = [spread(inv[top], row + j) for j in range(wide)]
+        times = [None] * wide
+        for j in range(wide):
+            root = lax.rsqrt(small[j][j])
+            one = 1.0 / small[j][j]
+            times[j] = [column * one for column in columns[j]]
+            times[j][0] = jnp.where(sub > row + j, times[j][0], 0.0)
+            old = jnp.ones((8, 128), F32) if scales[top] is None else scales[top]
+            scales[top] = jnp.where(sub == row + j, root, old)
+            for i in range(j + 1, wide):
+                factor = small[i][j] * one
+                pivot_rows[i] = pivot_rows[i] - factor * pivot_rows[j]
+                inv_rows[i] = inv_rows[i] - factor * inv_rows[j]
+                for k in range(i, wide):
+                    small[k][i] = small[k][i] - factor * small[k][j]
+                columns[i] = [a - b * small[i][j] for a, b in zip(columns[i], times[j])]
+        for g in range(top, groups):
+            for j in range(wide):
+                left[g] = left[g] - times[j][g - top] * pivot_rows[j]
+                inv[g] = inv[g] - times[j][g - top] * inv_rows[j]
+    return jnp.concatenate([inv[g] * scales[g] for g in range(groups)], axis=0)
+
+
+def factor_kernel(scale, rows_in, gram_in, basis_ref, chol_ref, rows_ref, gram_ref, sems):
+    fetch_gram = pltpu.make_async_copy(gram_in, gram_ref, sems.at[0])
+    fetch_rows = pltpu.make_async_copy(rows_in, rows_ref, sems.at[1])
+    fetch_gram.start()
+    fetch_rows.start()
+    fetch_gram.wait()
     rank = gram_ref.shape[1]
     tiles = gram_ref.shape[0] // rank
     size = 128 // tiles
-    lane = lax.broadcasted_iota(jnp.int32, (size, 128), 1)
-    sub = lax.broadcasted_iota(jnp.int32, (size, 128), 0)
-    first = (lane // size) * size
-    unit = (lane - first == sub).astype(F32)
 
     def dott(a, b):
         return lax.dot_general(a, b, (((1,), (1,)), ((), ())), precision=HIGHEST,
@@ -334,16 +391,7 @@
     done = [[] for _ in range(tiles)]
     for b in range(rank // size):
         packed = jnp.concatenate([trail[t][:size, :size] for t in range(tiles)], axis=1)
-        inv = unit
-        pivots = jnp.ones((size, 128), F32)
-        for k in range(size):
-            column = jnp.take_along_axis(packed, first + k, axis=1)
-            pivot = column[k:k + 1, :]
-            times = jnp.where(sub > k, column / pivot, 0.0)
-            pivots = jnp.where(sub == k, pivot, pivots)
-            packed = packed - times * packed[k:k + 1, :]
-            inv = inv - times * inv[k:k + 1, :]
-        inv = inv * lax.rsqrt(pivots)
+        inv = eliminate(packed, size, 8)
         for t in range(tiles):
             small = inv[:, t * size:(t + 1) * size]
             head = dot(small, rest_inv[t][:size, :])
@@ -354,6 +402,7 @@
                 rest_inv[t] = rest_inv[t][size:, :] - dot(below, head)
     row = lax.broadcasted_iota(jnp.int32, (rank, rank), 0)
     col = lax.broadcasted_iota(jnp.int32, (rank, rank), 1)
+    fetch_rows.wait()
     for t in range(tiles):
         inverse = jnp.concatenate(done[t], axis=0)
         basis_ref[t] = dott(rows_ref[:, t * rank:(t + 1) * rank], inverse) * scale
@@ -376,8 +425,9 @@
         out_shape=(jax.ShapeDtypeStruct((own_rows, listed * rank), F32),
                    jax.ShapeDtypeStruct((listed, rank, rank), F32)),
         in_specs=[pl.BlockSpec(memory_space=pltpu.SMEM), hbm, hbm, hbm],
-        out_specs=(vmem, vmem),
+        out_specs=(hbm, hbm),
         scratch_shapes=[
+            pltpu.VMEM((own_rows, listed * rank), F32),
             pltpu.VMEM((panels, size, rank), BF16), pltpu.VMEM((size, rank), BF16),
             pltpu.VMEM((ys, rows, rank), BF16), pltpu.VMEM((ys, rows, rank), BF16),
             pltpu.VMEM((ys, panels, rank, rank), BF16),
@@ -397,12 +447,12 @@
             dma((panels, number)), dma((panels, 2, 2, ysteps)), dma((panels, 2, 2, ysteps)),
             dma((2, zs)), dma((2, zs)), dma((listed, 2, zsteps)), dma((listed, 2, zsteps)),
             dma((2,)), dma((2,)), dma((2, zs)), dma((2, zs)), dma((2, zs)), dma((2, zs)),
-            dma((2,)), dma((2,)),
+            dma((2,)), dma((2,)), dma, dma((listed,)),
         ],
         compiler_params=pltpu.CompilerParams(
             collective_id=0, has_side_effects=True, vmem_limit_bytes=56 * 2 ** 20),
         name="updates",
-    )(tile_list, left, right, probe)
+    )(jnp.transpose(tile_list), left, right, probe)
 
 
 def factors(rows, gram, scale):
@@ -410,13 +460,16 @@
     rank = gram.shape[1]
     tiles = width // rank
     vmem = pl.BlockSpec(memory_space=pltpu.VMEM)
+    hbm = pl.BlockSpec(memory_space=pl.ANY)
     return pl.pallas_call(
         functools.partial(factor_kernel, scale),
         out_shape=(jax.ShapeDtypeStruct((tiles, size, rank), F32),
                    jax.ShapeDtypeStruct((tiles, rank, rank), F32)),
-        in_specs=[vmem, vmem],
+        in_specs=[hbm, hbm],
         out_specs=(vmem, vmem),
-        compiler_params=pltpu.CompilerParams(vmem_limit_bytes=40 * 2 ** 20),
+        scratch_shapes=[pltpu.VMEM((size, width), F32), pltpu.VMEM((tiles * rank, rank), F32),
+                        pltpu.SemaphoreType.DMA((2,))],
+        compiler_params=pltpu.CompilerParams(vmem_limit_bytes=60 * 2 ** 20),
         name="factors",
     )(rows, gram)
 

time: 133 us -> 120 us (0.902)
  Pallas kernels: 129 us -> 119 us
  local copies, waits for them, and re-layouts: 3.26 us -> 0 us
    pallas_call x1, Pallas kernels: 16.8 us -> 10.4 us  [factors(): pl.pallas_call(functools.partial(factor_kernel, scale), out_shape=(jax.Sh...]
    unnamed x7 -> x0, local copies, waits for them, and re-layouts: 3.26 us -> none
    pallas_call x1, Pallas kernels: 112 us -> 109 us  [updates(): pl.pallas_call(functools.partial(update_kernel, xs, ys, zs), out_shape=(j...]
where the time goes in v3:
time: 120 us
  Pallas kernels  119 us (99%)
    pallas_call x1, Pallas kernels, updates(): pl.pallas_call(functools.partial(update_kernel, xs, ys, zs), out_shape=(j...  109 us
    pallas_call x1, Pallas kernels, factors(): pl.pallas_call(functools.partial(factor_kernel, scale), out_shape=(jax.Sh...  10.4 us

profile of v3, /device:TPU:1, one launch (start us, length us, event | category | flops | bytes accessed | tf_op | source)
XLA Modules:
  0.0 119.9 jit_solution(12666762481154931629)
XLA Ops:
  0.6 108.9 %updates.1 = (f32[128,512]{1,0:T(8,128)}, f32[4,128,128]{2,1,0:T(8,128)}) custom-call(s32[4,32]{1,0:T(4,128)} %bitcast.9, bf16[2,2048,128]{2,1,0:T(8,128)(2,1)} %bitcast.6, bf16[2,2048,128]{2,1,0:T(8,128)(2,1)} %bitcast.7, bf16[2048,128]{1,0:T(8,128)(2,1)} %om_ref.1), custom_call_target="tpu_custom_call" | custom-call | tf_op jit(solution)/shard_map/updates/pallas_call | solution.py:423
  109.5 10.4 %factors.1 = (f32[4,128,128]{2,1,0:T(8,128)}, f32[4,128,128]{2,1,0:T(8,128)}) custom-call(f32[128,512]{1,0:T(8,128)} %get-tuple-element.6.rows_in, f32[512,128]{1,0:T(8,128)} %bitcast.8), custom_call_target="tpu_custom_call" | custom-call | tf_op jit(solution)/shard_map/factors/pallas_call | solution.py:464

commit v4 on v3

--- a/solution.py
+++ b/solution.py
@@ -28,10 +28,10 @@
 
 
 def update_kernel(xs, ys, zs, tile_ref, u_ref, v_ref, om_ref, rows_out, gram_out,
-                  rows_ref, uv, om, vb0, vb1, ma, sa0, sa1, stage, rbuf, cpl,
-                  xsend, xrecv, held, zstage, zbuf, gpart, gx, ghalf, gr, gall, gout,
+                  rows_ref, uv, uo, om, vb0, vb1, ma, sa0, sa1, stage, rbuf, cpl,
+                  cpo, held, zstage, zbuf, gpart, gx, ghalf, gr, gall, gout,
                   u_sem, om_sem, own_sem, v_send, v_recv, m_send, m_recv,
-                  s_send, f_send, s_recv, r_send, r_recv, x_send, x_recv,
+                  s_send, f_send, s_recv, r_send, r_recv, u_send, u_recv, x_send, x_recv,
                   z_send, z_recv, g_send, g_recv, a_send, a_recv, b_send, b_recv,
                   e_send, e_recv, rows_sem, tile_sem):
     vb, sa = (vb0, vb1), (sa0, sa1)
@@ -95,7 +95,7 @@
     om_copy.wait()
     for p in range(panels):
         u_copies[p].wait()
-        ma[y, p] = tdot(uv[p], om[...]).astype(BF16)
+        ma[y, p] = tdot(uv[p].reshape(om.shape), om[...]).astype(BF16)
     pl.semaphore_wait(barrier, len(greet))
 
     m_reach = {1: ys // 2, -1: ys - 1 - ys // 2}
@@ -174,22 +174,16 @@
         far += [away, -away]
     far.append(0)
 
-    def term_rows(h, zd, cd):
-        start = pl.multiple_of((zd * CORES + cd) * own_rows, own_rows)
-        left = jnp.concatenate([uv[p, pl.ds(start, own_rows), :] for p in range(panels)], axis=1)
-        return jnp.dot(left, cpl[h], preferred_element_type=F32)
-
     def give(h):
-        for dz in far:
-            zd = zat(dz)
-            xsend[h, zd] = term_rows(h, zd, 1 - c).astype(BF16)
-            send(xsend.at[h, zd], xrecv.at[h, zd], x_send.at[h, zd], x_recv.at[h, zd], partner)
+        send(cpl.at[h], cpo.at[h], x_send.at[h], x_recv.at[h], partner)
+        wait_in(cpo.at[h], x_recv.at[h])
 
     def take(h, dz):
         zd = zat(dz)
-        mine = term_rows(h, zd, c)
-        wait_in(xrecv.at[h, zd], x_recv.at[h, zd])
-        held[h, zd] = mine + xrecv[h, zd].astype(F32)
+        left = jnp.concatenate([uv[p, zd, c] for p in range(panels)]
+                               + [uo[p, zd] for p in range(panels)], axis=1)
+        both = jnp.concatenate([cpl[h], cpo[h]], axis=0)
+        held[h, zd] = jnp.dot(left, both, preferred_element_type=F32)
 
     def held_tile(h, k, dz):
         return held[h, zat(dz), :, k * rank:(k + 1) * rank]
@@ -287,6 +281,7 @@
     send_m(y, -1)
     for _ in range(4):
         send_next()
+    send(u_ref.at[:, :, 1 - c], uo, u_send, u_recv, partner)
     late = []
     for turn in turns:
         sketch_block(*turn)
@@ -303,6 +298,7 @@
         for h in range(halves):
             for p in range(panels):
                 ring_step(p, h, s)
+    wait_in(uo, u_recv)
     for h in range(halves):
         for p in range(panels):
             ring_end(p, h)
@@ -428,14 +424,15 @@
         out_specs=(hbm, hbm),
         scratch_shapes=[
             pltpu.VMEM((own_rows, listed * rank), F32),
-            pltpu.VMEM((panels, size, rank), BF16), pltpu.VMEM((size, rank), BF16),
+            pltpu.VMEM((panels, zs, CORES, own_rows, rank), BF16),
+            pltpu.VMEM((panels, zs, own_rows, rank), BF16), pltpu.VMEM((size, rank), BF16),
             pltpu.VMEM((ys, rows, rank), BF16), pltpu.VMEM((ys, rows, rank), BF16),
             pltpu.VMEM((ys, panels, rank, rank), BF16),
             pltpu.VMEM((number, rows, rank), BF16), pltpu.VMEM((number, rows, rank), BF16),
             pltpu.VMEM((panels, 2, 2, ysteps, rank, width), BF16),
             pltpu.VMEM((panels, 2, 2, ysteps, rank, width), BF16),
             pltpu.VMEM((2, panels * rank, width), BF16),
-            pltpu.VMEM((2, zs, own_rows, width), BF16), pltpu.VMEM((2, zs, own_rows, width), BF16),
+            pltpu.VMEM((2, panels * rank, width), BF16),
             pltpu.VMEM((2, zs, own_rows, width), F32),
             pltpu.VMEM((listed, 2, zsteps, own_rows, rank), BF16),
             pltpu.VMEM((listed, 2, zsteps, own_rows, rank), BF16),
@@ -445,14 +442,14 @@
             dma((panels,)), dma, dma((panels,)), dma((panels, ys)), dma((panels, ys)),
             dma((ys, 2)), dma((ys,)), dma((panels, 2, ys)), dma((panels, ys)),
             dma((panels, number)), dma((panels, 2, 2, ysteps)), dma((panels, 2, 2, ysteps)),
-            dma((2, zs)), dma((2, zs)), dma((listed, 2, zsteps)), dma((listed, 2, zsteps)),
+            dma, dma, dma((2,)), dma((2,)), dma((listed, 2, zsteps)), dma((listed, 2, zsteps)),
             dma((2,)), dma((2,)), dma((2, zs)), dma((2, zs)), dma((2, zs)), dma((2, zs)),
             dma((2,)), dma((2,)), dma, dma((listed,)),
         ],
         compiler_params=pltpu.CompilerParams(
             collective_id=0, has_side_effects=True, vmem_limit_bytes=56 * 2 ** 20),
         name="updates",
-    )(jnp.transpose(tile_list), left, right, probe)
+    )(jnp.transpose(tile_list), left.reshape(panels, zs, CORES, own_rows, rank), right, probe)
 
 
 def factors(rows, gram, scale):

time: 120 us -> 119 us (level)
  no operation moved by 1% of the time
where the time goes in v4:
time: 119 us
  Pallas kernels  118 us (99%)
    pallas_call x1, Pallas kernels, updates(): pl.pallas_call(functools.partial(update_kernel, xs, ys, zs), out_shape=(j...  108 us
    pallas_call x1, Pallas kernels, factors(): pl.pallas_call(functools.partial(factor_kernel, scale), out_shape=(jax.Sh...  10.4 us

profile of v4, /device:TPU:1, one launch (start us, length us, event | category | flops | bytes accessed | tf_op | source)
XLA Modules:
  0.0 118.9 jit_solution(13028296649084220607)
XLA Ops:
  0.6 107.9 %updates.1 = (f32[128,512]{1,0:T(8,128)}, f32[4,128,128]{2,1,0:T(8,128)}) custom-call(s32[4,32]{1,0:T(4,128)} %bitcast.9, bf16[2,8,2,128,128]{4,3,2,1,0:T(8,128)(2,1)} %bitcast.6, bf16[2,2048,128]{2,1,0:T(8,128)(2,1)} %bitcast.7, bf16[2048,128]{1,0:T(8,128)(2,1)} %om_ref.1), custom_call_target="tpu_custom_call" | custom-call | tf_op jit(solution)/shard_map/updates/pallas_call | solution.py:419
  108.5 10.4 %factors.1 = (f32[4,128,128]{2,1,0:T(8,128)}, f32[4,128,128]{2,1,0:T(8,128)}) custom-call(f32[128,512]{1,0:T(8,128)} %get-tuple-element.6.rows_in, f32[512,128]{1,0:T(8,128)} %bitcast.8), custom_call_target="tpu_custom_call" | custom-call | tf_op jit(solution)/shard_map/factors/pallas_call | solution.py:461

commit v5 on v4

--- a/solution.py
+++ b/solution.py
@@ -363,6 +363,16 @@
     return jnp.concatenate([inv[g] * scales[g] for g in range(groups)], axis=0)
 
 
+def dot_halves(a, b):
+    a_high, b_high = a.astype(BF16), b.astype(BF16)
+    a_low = (a - a_high.astype(F32)).astype(BF16)
+    b_low = (b - b_high.astype(F32)).astype(BF16)
+    return lax.dot_general(
+        jnp.concatenate([a_high, a_high, a_low], axis=1),
+        jnp.concatenate([b_high, b_low, b_high], axis=1),
+        (((1,), (1,)), ((), ())), preferred_element_type=F32)
+
+
 def factor_kernel(scale, rows_in, gram_in, basis_ref, chol_ref, rows_ref, gram_ref, sems):
     fetch_gram = pltpu.make_async_copy(gram_in, gram_ref, sems.at[0])
     fetch_rows = pltpu.make_async_copy(rows_in, rows_ref, sems.at[1])
@@ -401,8 +411,8 @@
     fetch_rows.wait()
     for t in range(tiles):
         inverse = jnp.concatenate(done[t], axis=0)
-        basis_ref[t] = dott(rows_ref[:, t * rank:(t + 1) * rank], inverse) * scale
-        lower = dott(gram_ref[t * rank:(t + 1) * rank, :], inverse)
+        basis_ref[t] = dot_halves(rows_ref[:, t * rank:(t + 1) * rank], inverse) * scale
+        lower = dot_halves(gram_ref[t * rank:(t + 1) * rank, :], inverse)
         chol_ref[t] = jnp.where(row >= col, lower * (1.0 / scale), 0.0)
 
 

time: 119 us -> 118 us (level)
  no operation moved by 1% of the time
where the time goes in v5:
time: 118 us
  Pallas kernels  118 us (100%)
    pallas_call x1, Pallas kernels, updates(): pl.pallas_call(functools.partial(update_kernel, xs, ys, zs), out_shape=(j...  108 us
    pallas_call x1, Pallas kernels, factors(): pl.pallas_call(functools.partial(factor_kernel, scale), out_shape=(jax.Sh...  9.6 us

profile of v5, /device:TPU:1, one launch (start us, length us, event | category | flops | bytes accessed | tf_op | source)
XLA Modules:
  0.0 118.1 jit_solution(15096481732701165860)
XLA Ops:
  0.6 107.9 %updates.1 = (f32[128,512]{1,0:T(8,128)}, f32[4,128,128]{2,1,0:T(8,128)}) custom-call(s32[4,32]{1,0:T(4,128)} %bitcast.9, bf16[2,8,2,128,128]{4,3,2,1,0:T(8,128)(2,1)} %bitcast.6, bf16[2,2048,128]{2,1,0:T(8,128)(2,1)} %bitcast.7, bf16[2048,128]{1,0:T(8,128)(2,1)} %om_ref.1), custom_call_target="tpu_custom_call" | custom-call | tf_op jit(solution)/shard_map/updates/pallas_call | solution.py:429
  108.5 9.6 %factors.1 = (f32[4,128,128]{2,1,0:T(8,128)}, f32[4,128,128]{2,1,0:T(8,128)}) custom-call(f32[128,512]{1,0:T(8,128)} %get-tuple-element.6.rows_in, f32[512,128]{1,0:T(8,128)} %bitcast.8), custom_call_target="tpu_custom_call" | custom-call | tf_op jit(solution)/shard_map/factors/pallas_call | solution.py:471
